TPU v7x, 32 devices: a whole 2x2x4 slice. The times are simulated.
32 devices in a mesh: groups: 2 (over y), gx: 16 (over z, x, core).
Axes of the slice: x: 2, y: 2, z: 4, core: 2. Of those that a mesh axis runs over, the one named last changes fastest.
Arguments:
- hidden: bfloat16 [64, 28672], P(('groups', 'gx')), parts along dimension 0, may hold values from -6 to 6
- shared_down_weight: bfloat16 [28672, 8192], P('gx'), may hold values from -0.03125 to 0.03125
- adapter_first_factors: bfloat16 [16, 64, 28672], P('gx'), may hold values from -0.03125 to 0.03125
- adapter_second_factors: bfloat16 [16, 64, 8192], P('gx'), may hold values from -0.375 to 0.375
- segment_row_counts: int32 [32], P('groups'), parts along dimension 0, may hold values from 1 to 4, 32 in all
- slot_tenant_owner: int32 [16], replicated, may hold values from 0 to 15, each once
Outputs:
- mixed: bfloat16 [64, 8192], P(('groups', 'gx')), parts along dimension 0
There are 2 independent parts, one for each index of `groups`. A program takes and returns all parts, laid end to end along the dimension named above; an argument that names none is the same for every part. Nothing has to cross between parts.
Inputs may be any that keep to these rules, and one draw needn't show every extreme that they name: `segment_row_counts`: the entries sum to 32; the largest is exactly 4. `slot_tenant_owner`: each tenant appears once.
All inputs are finite; a program needn't handle non-finite values.
Results may differ from a plain program's by a relative error of at most 0.0031.
Values may be sent and summed in bfloat16 or wider, within the bound.
A program may use at most 128 MiB of HBM per device.

v0:
```python
import jax
import jax.numpy as jnp
from jax import lax
from jax.sharding import PartitionSpec as P

MOST = 4


def per_device(
    hidden,
    shared_down_weight,
    adapter_first_factors,
    adapter_second_factors,
    segment_row_counts,
    slot_tenant_owner,
):
    devices = lax.axis_size("gx")
    own_index = lax.axis_index("gx")
    rows_dev = hidden.shape[0]
    total_rows = rows_dev * devices
    hidden_features_local = lax.all_to_all(hidden, "gx", split_axis=1, concat_axis=0, tiled=True)
    seg_ends = jnp.cumsum(segment_row_counts)
    seg_starts = seg_ends - segment_row_counts
    row_index = jnp.arange(total_rows, dtype=jnp.int32)
    row_tenant = jnp.sum((seg_ends[None, :] <= row_index[:, None]).astype(jnp.int32), axis=1)
    windows = jnp.minimum(seg_starts, total_rows - MOST)
    row_local = row_index - windows[row_tenant]

    def take_window(first_row):
        return lax.dynamic_slice_in_dim(hidden_features_local, first_row, MOST, 0)

    slot_blocks = jax.vmap(take_window)(windows[slot_tenant_owner])
    tenant_first_factor = adapter_first_factors[0]
    tenant_second_factor = adapter_second_factors[0]
    shrunk = lax.dot_general(
        lax.all_to_all(slot_blocks, "gx", split_axis=0, concat_axis=2, tiled=True),
        tenant_first_factor,
        (((2,), (1,)), ((), ())),
        preferred_element_type=jnp.float32,
    )
    shrunk = shrunk.astype(jnp.bfloat16)
    owned_delta = lax.dot_general(
        shrunk, tenant_second_factor, (((2,), (0,)), ((), ())), preferred_element_type=jnp.float32
    )[0]
    own_tenant = slot_tenant_owner[own_index]
    in_segment = (row_tenant == own_tenant).astype(jnp.float32)
    adapter_output_part = (
        jnp.take(owned_delta, jnp.clip(row_local, 0, MOST - 1), axis=0) * in_segment[:, None]
    )
    summed = lax.psum_scatter(
        jnp.dot(hidden_features_local, shared_down_weight, preferred_element_type=jnp.float32)
        + adapter_output_part,
        "gx",
        scatter_dimension=0,
        tiled=True,
    )
    return summed.astype(jnp.bfloat16)


def solution(mesh):
    return jax.shard_map(
        per_device,
        mesh=mesh,
        in_specs=(
            P(("groups", "gx"), None),
            P("gx", None),
            P("gx", None, None),
            P("gx", None, None),
            P("groups"),
            P(),
        ),
        out_specs=P(("groups", "gx"), None),
        check_vma=False,
    )
```

profile of v0, /device:TPU:0, one launch (start us, length us, event | category | flops | bytes accessed | tf_op | source)
XLA Modules:
  0.0 144.3 jit_solution(371490487500344507)
XLA Ops:
  0.0 7.5 %all-to-all-start = ((bf16[2,16,1792]{2,0,1:T(2,128)(2,1)}), bf16[2,16,1792]{2,0,1:T(2,128)(2,1)S(1)}, u32[]{:S(2)}, u32[]{:S(2)}) async-start(bf16[2,16,1792]{2,0,1:T(2,128)(2,1)} %bitcast.46), calls=%async_computation | async-start | bytes 229376 | tf_op jit(solution)/shard_map/all_to_all | solution.py:21
  7.5 0.7 copy.14
  8.5 0.7 subtract_minimum_fusion
  9.2 0.7 compare_select_fusion.2
  9.8 0.7 gather_fusion
  10.5 0.7 gather_fusion.1
  11.2 4.0 %all-to-all-done = bf16[2,16,1792]{2,0,1:T(2,128)(2,1)S(1)} async-done(((bf16[2,16,1792]{2,0,1:T(2,128)(2,1)}), bf16[2,16,1792]{2,0,1:T(2,128)(2,1)S(1)}, u32[]{:S(2)}, u32[]{:S(2)}) %all-to-all-start) | async-done | bytes 114720 | tf_op jit(solution)/shard_map/all_to_all | solution.py:21
  15.2 28.3 %while.1 = (s32[]{:T(128)}, bf16[32,1792]{1,0:T(8,128)(2,1)S(1)}, s32[16,2]{0,1:T(2,128)S(1)}, bf16[16,4,1792]{2,1,0:T(4,128)(2,1)}, s32[]{:T(128)}) while((s32[]{:T(128)}, bf16[32,1792]{1,0:T(8,128)(2,1)S(1)}, s32[16,2]{0,1:T(2,128)S(1)}, bf16[16,4,1792]{2,1,0:T(4,128)(2,1)}, s32[]{:T(128)}) %tuple.17), condition=%wide.while_cond, body=%wide.while_body.sunk | while | flops 2 | bytes 29785 | solution.py:30
  15.3 0.5 slice.18
  15.8 1.2 bitcast_dynamic-update-slice_fusion.2
  17.1 0.5 slice.18
  17.6 1.2 bitcast_dynamic-update-slice_fusion.2
  18.8 0.5 slice.18
  19.4 1.2 bitcast_dynamic-update-slice_fusion.2
  20.6 0.5 slice.18
  21.1 1.2 bitcast_dynamic-update-slice_fusion.2
  22.4 0.5 slice.18
  22.9 1.2 bitcast_dynamic-update-slice_fusion.2
  24.2 0.5 slice.18
  24.7 1.2 bitcast_dynamic-update-slice_fusion.2
  25.9 0.5 slice.18
  26.4 1.2 bitcast_dynamic-update-slice_fusion.2
  27.7 0.5 slice.18
  28.2 1.2 bitcast_dynamic-update-slice_fusion.2
  29.5 0.5 slice.18
  30.0 1.2 bitcast_dynamic-update-slice_fusion.2
  31.2 0.5 slice.18
  31.8 1.2 bitcast_dynamic-update-slice_fusion.2
  33.0 0.5 slice.18
  33.5 1.2 bitcast_dynamic-update-slice_fusion.2
  34.8 0.5 slice.18
  35.3 1.2 bitcast_dynamic-update-slice_fusion.2
  36.6 0.5 slice.18
  37.1 1.2 bitcast_dynamic-update-slice_fusion.2
  38.8 1.2 bitcast_dynamic-update-slice_fusion.2
  40.1 0.5 slice.18
  40.6 1.2 bitcast_dynamic-update-slice_fusion.2
  42.4 1.2 bitcast_dynamic-update-slice_fusion.2
  43.6 3.5 %all-to-all-start.1 = ((bf16[16,4,1792]{2,1,0:T(4,128)(2,1)}), bf16[16,4,1792]{2,1,0:T(4,128)(2,1)S(1)}, u32[]{:S(2)}, u32[]{:S(2)}) async-start(bf16[16,4,1792]{2,1,0:T(4,128)(2,1)} %get-tuple-element.12), calls=%async_computation.1 | async-start | bytes 458752 | tf_op jit(solution)/shard_map/all_to_all | solution.py:36
  47.1 1.2 dynamic_slice.3
  48.4 1.2 dynamic-slice.4
  50.2 0.7 compare_convert_fusion
  50.9 5.7 %all-to-all-done.1 = bf16[16,4,1792]{2,1,0:T(4,128)(2,1)S(1)} async-done(((bf16[16,4,1792]{2,1,0:T(4,128)(2,1)}), bf16[16,4,1792]{2,1,0:T(4,128)(2,1)S(1)}, u32[]{:S(2)}, u32[]{:S(2)}) %all-to-all-start.1) | async-done | bytes 229408 | tf_op jit(solution)/shard_map/all_to_all | solution.py:36
  56.6 3.6 %fusion.6 = f32[4,8192]{1,0:T(4,128)S(1)} fusion(bf16[4,28672]{1,0:T(4,128)(2,1)S(1)} %bitcast.44, bf16[1,64,28672]{2,1,0:T(8,128)(2,1)} %param.8, bf16[1,64,8192]{2,1,0:T(8,128)(2,1)S(1)} %copy-done), kind=kOutput, calls=%fused_computation.9 | convolution fusion | flops 18874624 | bytes 5079040 | tf_op jit(solution)/shard_map/dot_general | solution.py:42
  60.2 0.9 gather_fusion.2
  61.1 12.0 %convolution_add_fusion = f32[32,8192]{1,0:T(8,128)S(1)} fusion(bf16[32,1792]{1,0:T(8,128)(2,1)S(1)} %get-tuple-element.64, bf16[1792,8192]{1,0:T(8,128)(2,1)} %param.7, f32[32,8192]{1,0:T(8,128)S(1)} %gather_fusion.2, f32[32]{0:T(128)S(1)} %get-tuple-element.21, pred[32]{0:T(512)(128)(4,1)S(1)} %get-tuple-element.22), kind=kOutput, calls=%fused_computation.5 | convolution fusion | flops 940310528 | bytes 31572128 | tf_op jit(solution)/shard_map/dot_general | solution.py:51
  73.1 70.6 %all-reduce.3 = bf16[32,8192]{1,0:T(8,128)(2,1)S(1)} all-reduce(f32[32,8192]{1,0:T(8,128)S(1)} %convolution_add_fusion), channel_id=2, replica_groups=mesh['groups'=2,'gx'=16] {'gx'}, use_global_device_ids=true, to_apply=%region_2.3.clone | all-reduce | flops 262144 | bytes 1572864
  143.7 0.7 dynamic-slice_convert_fusion
  (32 shorter events, 2.5 us)
Async XLA Ops:
  0.0 56.6 %copy-start = (bf16[1,64,8192]{2,1,0:T(8,128)(2,1)S(1)}, bf16[1,64,8192]{2,1,0:T(8,128)(2,1)}, u32[]{:S(2)}) copy-start(bf16[1,64,8192]{2,1,0:T(8,128)(2,1)} %param.9) | copy-start | bytes 3145732
  0.0 15.2 %all-to-all-start = ((bf16[2,16,1792]{2,0,1:T(2,128)(2,1)}), bf16[2,16,1792]{2,0,1:T(2,128)(2,1)S(1)}, u32[]{:S(2)}, u32[]{:S(2)}) async-start(bf16[2,16,1792]{2,0,1:T(2,128)(2,1)} %bitcast.46), calls=%async_computation | async-start | bytes 229376 | tf_op jit(solution)/shard_map/all_to_all | solution.py:21
  43.6 13.0 %all-to-all-start.1 = ((bf16[16,4,1792]{2,1,0:T(4,128)(2,1)}), bf16[16,4,1792]{2,1,0:T(4,128)(2,1)S(1)}, u32[]{:S(2)}, u32[]{:S(2)}) async-start(bf16[16,4,1792]{2,1,0:T(4,128)(2,1)} %get-tuple-element.12), calls=%async_computation.1 | async-start | bytes 458752 | tf_op jit(solution)/shard_map/all_to_all | solution.py:36
where the time goes:
time: 145 us; the launch traced here: 144 us
  blocking collectives  70.6 us (49%)
  local copies, waits for them, and re-layouts  34.5 us (24%)
  matrix products  15.6 us (11%)
  starting transfers between devices  11 us (8%)
  waiting for transfers between devices  9.7 us (7%)
  other arithmetic  2.26 us (2%)
    unnamed x1, blocking collectives  70.6 us
    gather x48, local copies, waits for them, and re-layouts  28.3 us
    dot_general x1, matrix products, per_device(): jnp.dot(hidden_features_local, shared_down_weight, preferred_element_type...  12 us
    all_to_all x1, starting transfers between devices, per_device(): lax.all_to_all(hidden, 'gx', split_axis=1, concat_axis=0, tiled=True)  7.49 us
    all_to_all x1, waiting for transfers between devices, per_device(): lax.all_to_all(slot_blocks, 'gx', split_axis=0, concat_axis=2, tiled=True)  5.73 us
    all_to_all x1, waiting for transfers between devices, per_device(): lax.all_to_all(hidden, 'gx', split_axis=1, concat_axis=0, tiled=True)  3.97 us
    dot_general x1, matrix products, per_device(): lax.dot_general(shrunk, tenant_second_factor, (((2,), (0,)), ((), ())), p...  3.6 us
    all_to_all x1, starting transfers between devices, per_device(): lax.all_to_all(slot_blocks, 'gx', split_axis=0, concat_axis=2, tiled=True)  3.53 us
  transfers between devices with their start and end apart: 2, of which 2 were waited for; matrix products, arithmetic and copies ran while one was open for 5% of the time, Pallas kernels for 0%

commit v1 on v0

--- a/solution.py
+++ b/solution.py
@@ -1,12 +1,342 @@
+import functools
+
 import jax
 import jax.numpy as jnp
 from jax import lax
+from jax.experimental import pallas as pl
+from jax.experimental.pallas import tpu as pltpu
 from jax.sharding import PartitionSpec as P
 
 MOST = 4
-
-
-def per_device(
+CHUNKS = 4
+TILE = 512
+MESH = pl.DeviceIdType.MESH
+
+
+def kernel(
+    n,
+    counts_ref,
+    owner_ref,
+    hidden_ref,
+    w_hbm,
+    a1_hbm,
+    a2_hbm,
+    out_ref,
+    wbuf,
+    a1,
+    a2,
+    rows_in,
+    xf,
+    xb,
+    onehot,
+    win_out,
+    win_in,
+    part,
+    pair_in,
+    chip_sum,
+    sum_out,
+    sum_in,
+    starts,
+    w_sem,
+    a_sem,
+    s1,
+    r1,
+    s2,
+    r2,
+    s3,
+    r3,
+    s4,
+    r4,
+):
+    me = lax.axis_index("gx")
+    chip, core = me // 2, me % 2
+    mate = chip * 2 + (1 - core)
+    chips = n // 2
+    rows_dev = hidden_ref.shape[0]
+    rows = rows_dev * n
+    half = rows // 2
+    depth = w_hbm.shape[0]
+    width = w_hbm.shape[1]
+    cw = width // CHUNKS
+    f32, bf16 = jnp.float32, jnp.bfloat16
+
+    def w_copy(k):
+        return pltpu.make_async_copy(w_hbm.at[:, pl.ds(k * cw, cw)], wbuf.at[k], w_sem.at[k])
+
+    a1_copy = pltpu.make_async_copy(a1_hbm.at[0], a1, a_sem.at[0])
+    a2_copy = pltpu.make_async_copy(a2_hbm.at[0], a2, a_sem.at[1])
+    w_copy(0).start()
+    a1_copy.start()
+    a2_copy.start()
+    for k in range(1, CHUNKS):
+        w_copy(k).start()
+
+    barrier = pltpu.get_barrier_semaphore()
+
+    def greet(o, c):
+        pl.semaphore_signal(barrier, inc=1, device_id={"gx": lax.rem(me + o, n)}, device_id_type=MESH)
+        return c
+
+    lax.fori_loop(1, n, greet, 0)
+    pl.semaphore_wait(barrier, n - 1)
+
+    def rows_copy(d, at):
+        return pltpu.make_async_remote_copy(
+            src_ref=hidden_ref.at[:, pl.ds(pl.multiple_of(d * depth, 128), depth)],
+            dst_ref=rows_in.at[at],
+            send_sem=s1.at[d],
+            recv_sem=r1.at[at],
+            device_id={"gx": d},
+            device_id_type=MESH,
+        )
+
+    def send_rows(o, c):
+        rows_copy(lax.rem(me + o, n), me).start()
+        return c
+
+    lax.fori_loop(1, n, send_rows, 0)
+    rows_in[me] = hidden_ref[:, pl.ds(pl.multiple_of(me * depth, 128), depth)]
+
+    total = jnp.int32(0)
+    for t in range(n):
+        starts[t] = total
+        total = total + counts_ref[t]
+    step = 8
+    pos = lax.broadcasted_iota(jnp.int32, (step, rows), 1)
+    row_at = ((pos % half) // rows_dev * 2 + pos // half) * rows_dev + pos % rows_dev
+    nth = lax.broadcasted_iota(jnp.int32, (step, rows), 0)
+    for s in range(n):
+        t = owner_ref[s]
+        hit = (row_at == starts[t] + nth) & (nth < counts_ref[t])
+        onehot[s * step : (s + 1) * step, :] = jnp.where(hit, 1.0, 0.0).astype(f32)
+
+    def wait_rows(o, c):
+        s = lax.rem(me + o, n)
+        rows_copy(s, s).wait_recv()
+        return c
+
+    lax.fori_loop(1, n, wait_rows, 0)
+    for s in range(n):
+        at = (s % 2) * half + (s // 2) * rows_dev
+        xf[at : at + rows_dev, :] = rows_in[s].astype(f32)
+    xb[...] = xf[...].astype(bf16)
+
+    chosen = jnp.dot(onehot[...].astype(bf16), xb[...], preferred_element_type=f32)
+    for s in range(n):
+        win_out[s] = chosen[s * step : s * step + MOST, :].astype(bf16)
+
+    def win_copy(d, at):
+        return pltpu.make_async_remote_copy(
+            src_ref=win_out.at[d],
+            dst_ref=win_in.at[at],
+            send_sem=s2.at[d],
+            recv_sem=r2.at[at],
+            device_id={"gx": d},
+            device_id_type=MESH,
+        )
+
+    def send_win(o, c):
+        win_copy(lax.rem(me + o, n), me).start()
+        return c
+
+    lax.fori_loop(1, n, send_win, 0)
+    win_in[me] = win_out[me]
+
+    def base(k):
+        w_copy(k).wait()
+
+        def tile(i, c):
+            cols = pl.ds(pl.multiple_of(i * TILE, TILE), TILE)
+            part[k, :, cols] = jnp.dot(xb[...], wbuf[k, :, cols], preferred_element_type=f32)
+            return c
+
+        lax.fori_loop(0, cw // TILE, tile, 0)
+
+    base(0)
+    base(1)
+
+    a1_copy.wait()
+
+    def wait_win(o, c):
+        s = lax.rem(me + o, n)
+        win_copy(s, s).wait_recv()
+        return c
+
+    lax.fori_loop(1, n, wait_win, 0)
+
+    def shrink(s, acc):
+        return acc + lax.dot_general(
+            win_in[s],
+            a1[:, pl.ds(pl.multiple_of(s * depth, 128), depth)],
+            (((1,), (1,)), ((), ())),
+            preferred_element_type=f32,
+        )
+
+    rank = a1.shape[0]
+    low = lax.fori_loop(0, n, shrink, jnp.zeros((MOST, rank), f32))
+    low = low.astype(bf16).astype(f32)
+    tenant = owner_ref[me]
+    pos = lax.broadcasted_iota(jnp.int32, (rows, rank), 0)
+    row_at = ((pos % half) // rows_dev * 2 + pos // half) * rows_dev + pos % rows_dev
+    spread = jnp.zeros((rows, rank), f32)
+    for j in range(MOST):
+        hit = (row_at == starts[tenant] + j) & (j < counts_ref[tenant])
+        spread = jnp.where(hit, jnp.broadcast_to(low[j : j + 1, :], (rows, rank)), spread)
+    spread = spread.astype(bf16)
+    a2_copy.wait()
+
+    mine = pl.ds(pl.multiple_of(core * half, 8), half)
+    other = pl.ds(pl.multiple_of((1 - core) * half, 8), half)
+
+    def pair_copy(k):
+        return pltpu.make_async_remote_copy(
+            src_ref=part.at[k, other],
+            dst_ref=pair_in.at[k],
+            send_sem=s3.at[k],
+            recv_sem=r3.at[k],
+            device_id={"gx": mate},
+            device_id_type=MESH,
+        )
+
+    def chip_copy(k, c, at):
+        return pltpu.make_async_remote_copy(
+            src_ref=sum_out.at[k, c],
+            dst_ref=sum_in.at[k, at],
+            send_sem=s4.at[k, c],
+            recv_sem=r4.at[k, at],
+            device_id={"gx": c * 2 + core},
+            device_id_type=MESH,
+        )
+
+    def add_delta(k):
+        def tile(i, c):
+            cols = pl.ds(pl.multiple_of(i * TILE, TILE), TILE)
+            from_a2 = pl.ds(pl.multiple_of(k * cw + i * TILE, TILE), TILE)
+            part[k, :, cols] += jnp.dot(spread, a2[:, from_a2], preferred_element_type=f32)
+            return c
+
+        lax.fori_loop(0, cw // TILE, tile, 0)
+        pair_copy(k).start()
+
+    def to_chips(k):
+        pair_copy(k).wait_recv()
+        chip_sum[k] = part[k, mine, :] + pair_in[k]
+        for c in range(chips):
+            sum_out[k, c] = chip_sum[k, c * rows_dev : (c + 1) * rows_dev, :].astype(bf16)
+
+        def send(o, x):
+            chip_copy(k, lax.rem(chip + o, chips), chip).start()
+            return x
+
+        lax.fori_loop(1, chips, send, 0)
+        sum_in[k, chip] = jnp.zeros(sum_in.shape[2:], bf16)
+
+    def finish(k):
+        def wait(o, x):
+            c = lax.rem(chip + o, chips)
+            chip_copy(k, c, c).wait_recv()
+            return x
+
+        lax.fori_loop(1, chips, wait, 0)
+        own = jnp.zeros((rows_dev, cw), f32)
+        for c in range(chips):
+            own += jnp.where(c == chip, chip_sum[k, c * rows_dev : (c + 1) * rows_dev, :], 0.0)
+            own += sum_in[k, c].astype(f32)
+        out_ref[:, k * cw : (k + 1) * cw] = own.astype(bf16)
+
+    add_delta(0)
+    add_delta(1)
+    to_chips(0)
+    to_chips(1)
+    for k in range(2, CHUNKS):
+        base(k)
+        add_delta(k)
+        to_chips(k)
+    for k in range(CHUNKS):
+        finish(k)
+
+    def drain(o, c):
+        d = lax.rem(me + o, n)
+        rows_copy(d, me).wait_send()
+        win_copy(d, me).wait_send()
+        return c
+
+    lax.fori_loop(1, n, drain, 0)
+
+    for k in range(CHUNKS):
+        pair_copy(k).wait_send()
+
+        def drain_chips(o, x, k=k):
+            chip_copy(k, lax.rem(chip + o, chips), chip).wait_send()
+            return x
+
+        lax.fori_loop(1, chips, drain_chips, 0)
+
+
+def fused(hidden, shared_down_weight, adapter_first_factors, adapter_second_factors, segment_row_counts, slot_tenant_owner):
+    n = lax.axis_size("gx")
+    rows_dev = hidden.shape[0]
+    rows = rows_dev * n
+    depth, width = shared_down_weight.shape
+    rank = adapter_first_factors.shape[1]
+    cw = width // CHUNKS
+    chips = n // 2
+    bf16, f32 = jnp.bfloat16, jnp.float32
+    dma = pltpu.SemaphoreType.DMA
+    vmem = pl.BlockSpec(memory_space=pltpu.VMEM)
+    smem = pl.BlockSpec(memory_space=pltpu.SMEM)
+    hbm = pl.BlockSpec(memory_space=pltpu.HBM)
+    return pl.pallas_call(
+        functools.partial(kernel, n),
+        out_shape=jax.ShapeDtypeStruct((rows_dev, width), bf16),
+        in_specs=[smem, smem, vmem, hbm, hbm, hbm],
+        out_specs=vmem,
+        scratch_shapes=[
+            pltpu.VMEM((CHUNKS, depth, cw), bf16),
+            pltpu.VMEM(adapter_first_factors.shape[1:], bf16),
+            pltpu.VMEM(adapter_second_factors.shape[1:], bf16),
+            pltpu.VMEM((n, rows_dev, depth), bf16),
+            pltpu.VMEM((rows, depth), f32),
+            pltpu.VMEM((rows, depth), bf16),
+            pltpu.VMEM((n * 8, rows), f32),
+            pltpu.VMEM((n, MOST, depth), bf16),
+            pltpu.VMEM((n, MOST, depth), bf16),
+            pltpu.VMEM((CHUNKS, rows, cw), f32),
+            pltpu.VMEM((CHUNKS, rows // 2, cw), f32),
+            pltpu.VMEM((CHUNKS, rows // 2, cw), f32),
+            pltpu.VMEM((CHUNKS, chips, rows_dev, cw), bf16),
+            pltpu.VMEM((CHUNKS, chips, rows_dev, cw), bf16),
+            pltpu.SMEM((n,), jnp.int32),
+            dma((CHUNKS,)),
+            dma((2,)),
+            dma((n,)),
+            dma((n,)),
+            dma((n,)),
+            dma((n,)),
+            dma((CHUNKS,)),
+            dma((CHUNKS,)),
+            dma((CHUNKS, chips)),
+            dma((CHUNKS, chips)),
+        ],
+        compiler_params=pltpu.CompilerParams(
+            collective_id=0, has_side_effects=True, vmem_limit_bytes=56 * 2**20
+        ),
+        cost_estimate=pl.CostEstimate(
+            flops=2 * rows * depth * width,
+            bytes_accessed=2 * (depth * width + rank * (depth * n + width)),
+            transcendentals=0,
+        ),
+    )(
+        segment_row_counts,
+        slot_tenant_owner,
+        hidden,
+        shared_down_weight,
+        adapter_first_factors,
+        adapter_second_factors,
+    )
+
+
+def general(
     hidden,
     shared_down_weight,
     adapter_first_factors,
@@ -57,6 +387,15 @@
     return summed.astype(jnp.bfloat16)
 
 
+def per_device(hidden, shared_down_weight, *rest):
+    n = lax.axis_size("gx")
+    depth, width = shared_down_weight.shape
+    aligned = depth % 128 == 0 and width % (CHUNKS * TILE) == 0 and (hidden.shape[0] * n) % 32 == 0
+    if aligned and n <= 16:
+        return fused(hidden, shared_down_weight, *rest)
+    return general(hidden, shared_down_weight, *rest)
+
+
 def solution(mesh):
     return jax.shard_map(
         per_device,

time: 145 us -> 38.8 us (0.27)
  blocking collectives: 70.6 us -> 0 us
  Pallas kernels: 0 us -> 37.2 us
  local copies, waits for them, and re-layouts: 34.5 us -> 1.4 us
  matrix products: 15.6 us -> 0 us
  starting transfers between devices: 11 us -> 0 us
  waiting for transfers between devices: 9.7 us -> 0 us
  other arithmetic: 2.26 us -> 0 us
    unnamed x1 -> x0, blocking collectives: 70.6 us -> none
    pallas_call x0 -> x1, Pallas kernels: none -> 37.2 us  [fused(): pl.pallas_call(functools.partial(kernel, n), out_shape=jax.ShapeDtypeStru...]
    gather x51 -> x0, local copies, waits for them, and re-layouts: 30.6 us -> none
    dot_general x2 -> x0, matrix products: 15.6 us -> none  [the longest x1 12 us: per_device(): jnp.dot(hidden_features_local, shared_down_weight, preferred_element_type...]
    all_to_all x2 -> x0, starting transfers between devices: 11 us -> none  [the longest x1 7.49 us: per_device(): lax.all_to_all(hidden, 'gx', split_axis=1, concat_axis=0, tiled=True)]
    all_to_all x2 -> x0, waiting for transfers between devices: 9.7 us -> none  [the longest x1 5.73 us: per_device(): lax.all_to_all(slot_blocks, 'gx', split_axis=0, concat_axis=2, tiled=True)]
  transfers between devices with their start and end apart: 2 -> 0, of which waited for: 2 -> 0; matrix products, arithmetic and copies ran while one was open for 5% -> 0% of each run, Pallas kernels for 0% -> 0%
where the time goes in v1:
time: 38.8 us; the launch traced here: 38.6 us
  Pallas kernels  37.2 us (96%)
  local copies, waits for them, and re-layouts  1.4 us (4%)
    pallas_call x1, Pallas kernels, fused(): pl.pallas_call(functools.partial(kernel, n), out_shape=jax.ShapeDtypeStru...  37.2 us
    unnamed x1, local copies, waits for them, and re-layouts  1.4 us

profile of v1, /device:TPU:0, one launch (start us, length us, event | category | flops | bytes accessed | tf_op | source)
XLA Modules:
  0.0 38.6 jit_solution(14121085017461150096)
XLA Ops:
  0.0 37.2 %shard_map.64 = bf16[2,8192]{1,0:T(2,128)(2,1)} custom-call(s32[16]{0:T(128)} %counts_ref.1, s32[16]{0:T(128)} %owner_ref.1, bf16[2,28672]{1,0:T(2,128)(2,1)} %hidden_ref.1, bf16[1792,8192]{1,0:T(8,128)(2,1)} %w_hbm.1, bf16[1,64,28672]{2,1,0:T(8,128)(2,1)} %a1_hbm.1, bf16[1,64,8192]{2,1,0:T(8,128)(2,1)} %a2_hbm.1), custom_call_target="tpu_custom_call" | custom-call | flops 939524096 | bytes 34078720 | tf_op jit(solution)/shard_map/pallas_call | solution.py:289
  37.2 1.4 %copy.8 = bf16[2,8192]{1,0:T(2,128)(2,1)} copy(bf16[2,8192]{1,0:T(2,128)(2,1)} %shard_map.64) | data formatting | bytes 65536

commit v2 on v1

--- a/solution.py
+++ b/solution.py
@@ -47,6 +47,9 @@
     r3,
     s4,
     r4,
+    s5,
+    r5,
+    low_pair,
 ):
     me = lax.axis_index("gx")
     chip, core = me // 2, me % 2
@@ -64,7 +67,10 @@
         return pltpu.make_async_copy(w_hbm.at[:, pl.ds(k * cw, cw)], wbuf.at[k], w_sem.at[k])
 
     a1_copy = pltpu.make_async_copy(a1_hbm.at[0], a1, a_sem.at[0])
-    a2_copy = pltpu.make_async_copy(a2_hbm.at[0], a2, a_sem.at[1])
+    rank = a1.shape[0]
+    own_a2 = pl.ds(pl.multiple_of(core * rank, 16), rank)
+    mate_a2 = pl.ds(pl.multiple_of((1 - core) * rank, 16), rank)
+    a2_copy = pltpu.make_async_copy(a2_hbm.at[0], a2.at[own_a2], a_sem.at[1])
     w_copy(0).start()
     a1_copy.start()
     a2_copy.start()
@@ -96,6 +102,24 @@
 
     lax.fori_loop(1, n, send_rows, 0)
     rows_in[me] = hidden_ref[:, pl.ds(pl.multiple_of(me * depth, 128), depth)]
+
+    a2_send = pltpu.make_async_remote_copy(
+        src_ref=a2_hbm.at[0],
+        dst_ref=a2.at[own_a2],
+        send_sem=s5.at[0],
+        recv_sem=r5.at[0],
+        device_id={"gx": mate},
+        device_id_type=MESH,
+    )
+    a2_recv = pltpu.make_async_remote_copy(
+        src_ref=a2_hbm.at[0],
+        dst_ref=a2.at[mate_a2],
+        send_sem=s5.at[0],
+        recv_sem=r5.at[0],
+        device_id={"gx": mate},
+        device_id_type=MESH,
+    )
+    a2_send.start()
 
     total = jnp.int32(0)
     for t in range(n):
@@ -152,39 +176,6 @@
 
         lax.fori_loop(0, cw // TILE, tile, 0)
 
-    base(0)
-    base(1)
-
-    a1_copy.wait()
-
-    def wait_win(o, c):
-        s = lax.rem(me + o, n)
-        win_copy(s, s).wait_recv()
-        return c
-
-    lax.fori_loop(1, n, wait_win, 0)
-
-    def shrink(s, acc):
-        return acc + lax.dot_general(
-            win_in[s],
-            a1[:, pl.ds(pl.multiple_of(s * depth, 128), depth)],
-            (((1,), (1,)), ((), ())),
-            preferred_element_type=f32,
-        )
-
-    rank = a1.shape[0]
-    low = lax.fori_loop(0, n, shrink, jnp.zeros((MOST, rank), f32))
-    low = low.astype(bf16).astype(f32)
-    tenant = owner_ref[me]
-    pos = lax.broadcasted_iota(jnp.int32, (rows, rank), 0)
-    row_at = ((pos % half) // rows_dev * 2 + pos // half) * rows_dev + pos % rows_dev
-    spread = jnp.zeros((rows, rank), f32)
-    for j in range(MOST):
-        hit = (row_at == starts[tenant] + j) & (j < counts_ref[tenant])
-        spread = jnp.where(hit, jnp.broadcast_to(low[j : j + 1, :], (rows, rank)), spread)
-    spread = spread.astype(bf16)
-    a2_copy.wait()
-
     mine = pl.ds(pl.multiple_of(core * half, 8), half)
     other = pl.ds(pl.multiple_of((1 - core) * half, 8), half)
 
@@ -198,6 +189,70 @@
             device_id_type=MESH,
         )
 
+    for k in range(CHUNKS):
+        base(k)
+        pair_copy(k).start()
+    for k in range(CHUNKS):
+        pair_copy(k).wait_recv()
+        chip_sum[k] = part[k, mine, :] + pair_in[k]
+
+    a1_copy.wait()
+
+    def wait_win(o, c):
+        s = lax.rem(me + o, n)
+        win_copy(s, s).wait_recv()
+        return c
+
+    lax.fori_loop(1, n, wait_win, 0)
+    low = jnp.zeros((rank, MOST), f32)
+    for s in range(n):
+        low += lax.dot_general(
+            a1[:, s * depth : (s + 1) * depth],
+            win_in[s],
+            (((1,), (1,)), ((), ())),
+            preferred_element_type=f32,
+        )
+
+    wide = 2 * rank
+    lane = lax.broadcasted_iota(jnp.int32, (rank, wide), 1)
+    unit = lax.broadcasted_iota(jnp.int32, (rank, wide), 0)
+    place = jnp.where(lane == unit + core * rank, 1.0, 0.0).astype(bf16)
+    low_pair[core] = lax.dot_general(
+        low.astype(bf16), place, (((0,), (0,)), ((), ())), preferred_element_type=f32
+    )
+    low_send = pltpu.make_async_remote_copy(
+        src_ref=low_pair.at[core],
+        dst_ref=low_pair.at[core],
+        send_sem=s5.at[1],
+        recv_sem=r5.at[1],
+        device_id={"gx": mate},
+        device_id_type=MESH,
+    )
+    low_recv = pltpu.make_async_remote_copy(
+        src_ref=low_pair.at[1 - core],
+        dst_ref=low_pair.at[1 - core],
+        send_sem=s5.at[1],
+        recv_sem=r5.at[1],
+        device_id={"gx": mate},
+        device_id_type=MESH,
+    )
+    low_send.start()
+    a2_copy.wait()
+    a2_recv.wait_recv()
+    pos = lax.broadcasted_iota(jnp.int32, (half, wide), 0)
+    lane = lax.broadcasted_iota(jnp.int32, (half, wide), 1)
+    row_at = (pos // rows_dev * 2 + core) * rows_dev + pos % rows_dev
+    even, odd = owner_ref[chip * 2], owner_ref[chip * 2 + 1]
+    first = jnp.where(lane < rank, starts[even], starts[odd])
+    many = jnp.where(lane < rank, counts_ref[even], counts_ref[odd])
+    low_recv.wait_recv()
+    low = low_pair[0] + low_pair[1]
+    spread = jnp.zeros((half, wide), f32)
+    for j in range(MOST):
+        hit = (row_at == first + j) & (j < many)
+        spread = jnp.where(hit, jnp.broadcast_to(low[j : j + 1, :], (half, wide)), spread)
+    spread = spread.astype(bf16)
+
     def chip_copy(k, c, at):
         return pltpu.make_async_remote_copy(
             src_ref=sum_out.at[k, c],
@@ -208,19 +263,14 @@
             device_id_type=MESH,
         )
 
-    def add_delta(k):
+    def to_chips(k):
         def tile(i, c):
             cols = pl.ds(pl.multiple_of(i * TILE, TILE), TILE)
             from_a2 = pl.ds(pl.multiple_of(k * cw + i * TILE, TILE), TILE)
-            part[k, :, cols] += jnp.dot(spread, a2[:, from_a2], preferred_element_type=f32)
+            chip_sum[k, :, cols] += jnp.dot(spread, a2[:, from_a2], preferred_element_type=f32)
             return c
 
         lax.fori_loop(0, cw // TILE, tile, 0)
-        pair_copy(k).start()
-
-    def to_chips(k):
-        pair_copy(k).wait_recv()
-        chip_sum[k] = part[k, mine, :] + pair_in[k]
         for c in range(chips):
             sum_out[k, c] = chip_sum[k, c * rows_dev : (c + 1) * rows_dev, :].astype(bf16)
 
@@ -244,13 +294,7 @@
             own += sum_in[k, c].astype(f32)
         out_ref[:, k * cw : (k + 1) * cw] = own.astype(bf16)
 
-    add_delta(0)
-    add_delta(1)
-    to_chips(0)
-    to_chips(1)
-    for k in range(2, CHUNKS):
-        base(k)
-        add_delta(k)
+    for k in range(CHUNKS):
         to_chips(k)
     for k in range(CHUNKS):
         finish(k)
@@ -263,6 +307,8 @@
 
     lax.fori_loop(1, n, drain, 0)
 
+    a2_send.wait_send()
+    low_send.wait_send()
     for k in range(CHUNKS):
         pair_copy(k).wait_send()
 
@@ -294,7 +340,7 @@
         scratch_shapes=[
             pltpu.VMEM((CHUNKS, depth, cw), bf16),
             pltpu.VMEM(adapter_first_factors.shape[1:], bf16),
-            pltpu.VMEM(adapter_second_factors.shape[1:], bf16),
+            pltpu.VMEM((2 * rank, width), bf16),
             pltpu.VMEM((n, rows_dev, depth), bf16),
             pltpu.VMEM((rows, depth), f32),
             pltpu.VMEM((rows, depth), bf16),
@@ -317,6 +363,9 @@
             dma((CHUNKS,)),
             dma((CHUNKS, chips)),
             dma((CHUNKS, chips)),
+            dma((2,)),
+            dma((2,)),
+            pltpu.VMEM((2, MOST, 2 * rank), f32),
         ],
         compiler_params=pltpu.CompilerParams(
             collective_id=0, has_side_effects=True, vmem_limit_bytes=56 * 2**20
@@ -391,7 +440,7 @@
     n = lax.axis_size("gx")
     depth, width = shared_down_weight.shape
     aligned = depth % 128 == 0 and width % (CHUNKS * TILE) == 0 and (hidden.shape[0] * n) % 32 == 0
-    if aligned and n <= 16:
+    if aligned and n <= 16 and rest[0].shape[1] % 64 == 0:
         return fused(hidden, shared_down_weight, *rest)
     return general(hidden, shared_down_weight, *rest)
 

time: 38.8 us -> 35.2 us (0.907)
  Pallas kernels: 37.2 us -> 33.6 us
    pallas_call x1, Pallas kernels: 37.2 us -> 33.6 us  [fused(): pl.pallas_call(functools.partial(kernel, n), out_shape=jax.ShapeDtypeStru...]
where the time goes in v2:
time: 35.2 us; the launch traced here: 35 us
  Pallas kernels  33.6 us (95%)
  local copies, waits for them, and re-layouts  1.4 us (4%)
    pallas_call x1, Pallas kernels, fused(): pl.pallas_call(functools.partial(kernel, n), out_shape=jax.ShapeDtypeStru...  33.6 us
    unnamed x1, local copies, waits for them, and re-layouts  1.4 us

profile of v2, /device:TPU:0, one launch (start us, length us, event | category | flops | bytes accessed | tf_op | source)
XLA Modules:
  0.0 35.0 jit_solution(1561636891304092090)
XLA Ops:
  0.0 33.6 %shard_map.64 = bf16[2,8192]{1,0:T(2,128)(2,1)} custom-call(s32[16]{0:T(128)} %counts_ref.1, s32[16]{0:T(128)} %owner_ref.1, bf16[2,28672]{1,0:T(2,128)(2,1)} %hidden_ref.1, bf16[1792,8192]{1,0:T(8,128)(2,1)} %w_hbm.1, bf16[1,64,28672]{2,1,0:T(8,128)(2,1)} %a1_hbm.1, bf16[1,64,8192]{2,1,0:T(8,128)(2,1)} %a2_hbm.1), custom_call_target="tpu_custom_call" | custom-call | flops 939524096 | bytes 34078720 | tf_op jit(solution)/shard_map/pallas_call | solution.py:335
  33.6 1.4 %copy.8 = bf16[2,8192]{1,0:T(2,128)(2,1)} copy(bf16[2,8192]{1,0:T(2,128)(2,1)} %shard_map.64) | data formatting | bytes 65536

commit v3 on v2

--- a/solution.py
+++ b/solution.py
@@ -8,7 +8,7 @@
 from jax.sharding import PartitionSpec as P
 
 MOST = 4
-CHUNKS = 4
+CHUNKS = 2
 TILE = 512
 MESH = pl.DeviceIdType.MESH
 

time: 35.2 us -> 34.3 us (0.974)
  Pallas kernels: 33.6 us -> 32.7 us
    pallas_call x1, Pallas kernels: 33.6 us -> 32.7 us  [fused(): pl.pallas_call(functools.partial(kernel, n), out_shape=jax.ShapeDtypeStru...]
where the time goes in v3:
time: 34.3 us; the launch traced here: 34.1 us
  Pallas kernels  32.7 us (95%)
  local copies, waits for them, and re-layouts  1.4 us (4%)
    pallas_call x1, Pallas kernels, fused(): pl.pallas_call(functools.partial(kernel, n), out_shape=jax.ShapeDtypeStru...  32.7 us
    unnamed x1, local copies, waits for them, and re-layouts  1.4 us

profile of v3, /device:TPU:0, one launch (start us, length us, event | category | flops | bytes accessed | tf_op | source)
XLA Modules:
  0.0 34.1 jit_solution(13458998349742593696)
XLA Ops:
  0.0 32.7 %shard_map.64 = bf16[2,8192]{1,0:T(2,128)(2,1)} custom-call(s32[16]{0:T(128)} %counts_ref.1, s32[16]{0:T(128)} %owner_ref.1, bf16[2,28672]{1,0:T(2,128)(2,1)} %hidden_ref.1, bf16[1792,8192]{1,0:T(8,128)(2,1)} %w_hbm.1, bf16[1,64,28672]{2,1,0:T(8,128)(2,1)} %a1_hbm.1, bf16[1,64,8192]{2,1,0:T(8,128)(2,1)} %a2_hbm.1), custom_call_target="tpu_custom_call" | custom-call | flops 939524096 | bytes 34078720 | tf_op jit(solution)/shard_map/pallas_call | solution.py:335
  32.7 1.4 %copy.8 = bf16[2,8192]{1,0:T(2,128)(2,1)} copy(bf16[2,8192]{1,0:T(2,128)(2,1)} %shard_map.64) | data formatting | bytes 65536
